TPU v7x, 256 devices: a whole 4x4x8 slice. The times are simulated.
256 devices in a mesh: dp: 32 (over z, y), mp: 8 (over x, core).
Axes of the slice: x: 4, y: 4, z: 8, core: 2. Of those that a mesh axis runs over, the one named last changes fastest.
Arguments:
- tokens: bfloat16 [12288, 4096], P(('dp', 'mp')), may hold values from -8 to 8
- encoded: bfloat16 [128, 128, 1024], P('dp'), may hold values from -8 to 8
- neighbour_owner: int32 [32, 6, 2], replicated, may hold values from 0 to 31, as said below
- neighbour_slot: int32 [32, 6, 2], replicated, may hold values from 0 to 3
- w_query: bfloat16 [4096, 4096], P(None, 'mp'), may hold values from -0.09375 to 0.09375
- w_key: bfloat16 [1024, 4096], P(None, 'mp'), may hold values from -0.1875 to 0.1875
- w_value: bfloat16 [1024, 4096], P(None, 'mp'), may hold values from -0.1875 to 0.1875
- w_out: bfloat16 [4096, 4096], P('mp'), may hold values from -0.09375 to 0.09375
- grad_out: bfloat16 [12288, 4096], P(('dp', 'mp')), may hold values from -6 to 6
Outputs:
- attended: bfloat16 [12288, 4096], P(('dp', 'mp'))
- grad_tokens: bfloat16 [12288, 4096], P(('dp', 'mp'))
- grad_encoded: float32 [128, 128, 1024], P('dp', None, 'mp')
Inputs may be any that keep to these rules, and one draw needn't show every extreme that they name: `neighbour_owner`: within one sequence's list no owner appears twice, and the list of sequence s names owner s.
All inputs are finite; a program needn't handle non-finite values.
Results may differ from a plain program's by a relative error of at most 0.017.
Values may be sent and summed in bfloat16 or wider, within the bound.
No kernel may reach another device: no remote copies, remote signals or barrier semaphores. Data moves between devices by JAX's collectives and lax.ppermute only.
A program may use at most 128 MiB of HBM per device.

v0:
```python
import math

import jax
import jax.numpy as jnp
from jax import lax
from jax.sharding import PartitionSpec as P

HD = 128
GROUP = 64
NBR = 2


def body(
    tokens, encoded, neighbour_owner, neighbour_slot, w_query, w_key, w_value, w_out, grad_out
):
    dp_count = lax.axis_size("dp")
    mp_count = lax.axis_size("mp")
    own_index = lax.axis_index("dp")
    score_scale = 1.0 / math.sqrt(HD)
    width = w_query.shape[1]
    heads_here = width // HD
    length = grad_out.shape[0] * mp_count
    group_count = length // GROUP
    neigh_count = group_count * NBR
    depth = encoded.shape[1]
    enc_width = encoded.shape[2]
    share = enc_width // mp_count
    owners_all = neighbour_owner.reshape(dp_count, neigh_count)
    slots_all = neighbour_slot.reshape(dp_count, neigh_count)
    held_here = owners_all == own_index
    wanted = jnp.any(held_here, axis=1)
    held_slot = jnp.sum(jnp.where(held_here, slots_all, 0), axis=1)
    my_owners = lax.dynamic_index_in_dim(owners_all, own_index, 0, keepdims=False)
    query = jnp.dot(
        lax.all_gather(tokens, "mp", axis=0, tiled=True),
        w_query,
        preferred_element_type=jnp.float32,
    ).astype(jnp.bfloat16)
    outgoing = jnp.where(wanted[:, None, None], encoded[held_slot], jnp.zeros((), jnp.bfloat16))
    arrived = lax.all_to_all(outgoing, "dp", split_axis=0, concat_axis=0, tiled=True)
    nearby = arrived[my_owners]
    flat_near = nearby.reshape(neigh_count * depth, enc_width)
    key_rows = jnp.dot(flat_near, w_key, preferred_element_type=jnp.float32).astype(jnp.bfloat16)
    value_rows = jnp.dot(flat_near, w_value, preferred_element_type=jnp.float32).astype(
        jnp.bfloat16
    )
    query_blocks = query.reshape(group_count, GROUP, heads_here, HD)
    key_blocks = key_rows.reshape(group_count, NBR * depth, heads_here, HD)
    value_blocks = value_rows.reshape(group_count, NBR * depth, heads_here, HD)
    scores = (
        jnp.einsum("cqhe,ckhe->chqk", query_blocks, key_blocks, preferred_element_type=jnp.float32)
        * score_scale
    )
    probs = jax.nn.softmax(scores, axis=-1)
    probs_b = probs.astype(jnp.bfloat16)
    heads_out = jnp.einsum(
        "chqk,ckhe->cqhe", probs_b, value_blocks, preferred_element_type=jnp.float32
    )
    heads_out = heads_out.astype(jnp.bfloat16).reshape(length, width)
    picked = heads_out
    attended = lax.psum_scatter(
        jnp.dot(picked, w_out, preferred_element_type=jnp.float32),
        "mp",
        scatter_dimension=0,
        tiled=True,
    ).astype(jnp.bfloat16)
    grad_heads = jnp.einsum(
        "td,hd->th",
        lax.all_gather(grad_out, "mp", axis=0, tiled=True),
        w_out,
        preferred_element_type=jnp.float32,
    ).astype(jnp.bfloat16)
    grad_blocks = grad_heads.reshape(group_count, GROUP, heads_here, HD)
    grad_probs = jnp.einsum(
        "cqhe,ckhe->chqk", grad_blocks, value_blocks, preferred_element_type=jnp.float32
    )
    centre = jnp.sum(probs * grad_probs, axis=-1, keepdims=True)
    grad_scores = (probs * (grad_probs - centre) * score_scale).astype(jnp.bfloat16)
    grad_query = jnp.einsum(
        "chqk,ckhe->cqhe", grad_scores, key_blocks, preferred_element_type=jnp.float32
    )
    grad_query = grad_query.astype(jnp.bfloat16).reshape(length, width)
    grad_keys = jnp.einsum(
        "chqk,cqhe->ckhe", grad_scores, query_blocks, preferred_element_type=jnp.float32
    )
    grad_keys = grad_keys.astype(jnp.bfloat16).reshape(neigh_count * depth, width)
    grad_values = jnp.einsum(
        "chqk,cqhe->ckhe", probs_b, grad_blocks, preferred_element_type=jnp.float32
    )
    grad_values = grad_values.astype(jnp.bfloat16).reshape(neigh_count * depth, width)
    picked = grad_query
    grad_tokens = lax.psum_scatter(
        jnp.einsum("td,ed->te", picked, w_query, preferred_element_type=jnp.float32),
        "mp",
        scatter_dimension=0,
        tiled=True,
    ).astype(jnp.bfloat16)
    grad_nearby = jnp.einsum("td,ed->te", grad_keys, w_key, preferred_element_type=jnp.float32)
    grad_nearby = grad_nearby + jnp.einsum(
        "td,ed->te", grad_values, w_value, preferred_element_type=jnp.float32
    )
    grad_nearby = grad_nearby.reshape(neigh_count, depth, enc_width)
    grad_share = lax.psum_scatter(
        grad_nearby.astype(jnp.bfloat16), "mp", scatter_dimension=2, tiled=True
    ).astype(jnp.float32)
    returning = jnp.zeros((dp_count, depth, share), jnp.float32).at[my_owners].set(grad_share)
    returned = lax.all_to_all(
        returning.astype(jnp.bfloat16), "dp", split_axis=0, concat_axis=0, tiled=True
    ).astype(returning.dtype)
    grad_encoded = (
        jnp.zeros((encoded.shape[0], depth, share), jnp.float32).at[held_slot].add(returned)
    )
    return (attended, grad_tokens, grad_encoded)


def solution(mesh):
    placed = (
        P(("dp", "mp"), None),
        P("dp", None, None),
        P(),
        P(),
        P(None, "mp"),
        P(None, "mp"),
        P(None, "mp"),
        P("mp", None),
        P(("dp", "mp"), None),
    )
    return jax.shard_map(
        body,
        mesh=mesh,
        in_specs=placed,
        out_specs=(P(("dp", "mp"), None), P(("dp", "mp"), None), P("dp", None, "mp")),
        check_vma=False,
    )
```

profile of v0, /device:TPU:8, one launch (start us, length us, event | category | flops | bytes accessed | tf_op | source)
XLA Modules:
  0.0 444.0 jit_solution(1037212377481915881)
XLA Ops:
  7.2 0.0 copy-start
  7.2 0.8 fusion.63
  8.0 0.7 select_reduce_fusion
  8.8 4.8 %gather_fusion = bf16[32,128,1024]{2,1,0:T(8,128)(2,1)} fusion(bf16[4,128,1024]{2,1,0:T(8,128)(2,1)S(1)} %copy-done, s32[1024]{0:T(1024)S(1)} %pad_clamp_fusion.1), kind=kCustom, calls=%fused_computation | custom fusion | bytes 16777344 | tf_op jit(solution)/shard_map/gather | solution.py:39
  13.6 7.2 %broadcast_select_fusion = bf16[32,128,1024]{2,1,0:T(8,128)(2,1)} fusion(bf16[32,128,1024]{2,1,0:T(8,128)(2,1)} %gather_fusion, pred[32]{0:T(512)(128)(4,1)S(1)} %fusion.63), kind=kLoop, calls=%fused_computation.6 | loop fusion | flops 4194304 | bytes 16777248 | tf_op jit(solution)/shard_map/jit(_where)/select_n | solution.py:39
  20.8 12.0 %all-to-all-start = ((bf16[32,128,1024]{2,1,0:T(8,128)(2,1)}), bf16[32,128,1024]{2,1,0:T(8,128)(2,1)}, u32[]{:S(2)}, u32[]{:S(2)}) async-start(bf16[32,128,1024]{2,1,0:T(8,128)(2,1)} %broadcast_select_fusion), calls=%async_computation | async-start | bytes 16777216 | tf_op jit(solution)/shard_map/all_to_all | solution.py:40
  32.8 0.0 all-gather.3.cloned.1.call-start
  32.8 0.7 all-gather.3.cloned.1.call-update
  33.5 0.0 all-gather.5.cloned.1.call-start
  33.6 0.7 all-gather.5.cloned.1.call-update
  34.3 0.0 reduce-scatter.10.cloned.1.call-start
  34.3 0.1 constant_dynamic-slice_fusion
  34.4 0.1 copy.49
  34.5 32.2 %all-gather.3.cloned.1.call-done = bf16[384,4096]{1,0:T(8,128)(2,1)} async-done(((bf16[48,4096]{1,0:T(8,128)(2,1)}), bf16[384,4096]{1,0:T(8,128)(2,1)}) %all-gather.3.cloned.1.call-update) | async-done | bytes 3145744 | tf_op jit(solution)/shard_map/all_gather | solution.py:35
  66.7 4.9 %convolution_convert_fusion.5 = bf16[384,512]{1,0:T(8,128)(2,1)S(1)} fusion(bf16[384,4096]{1,0:T(8,128)(2,1)} %all-gather.3.cloned.1.call-done, bf16[4096,512]{1,0:T(8,128)(2,1)} %param.13), kind=kOutput, calls=%fused_computation.36 | convolution fusion | flops 1610809344 | bytes 7733248 | tf_op jit(solution)/shard_map/dot_general | solution.py:34
  71.7 0.1 reshape.87
  71.8 27.2 %all-gather.5.cloned.1.call-done = bf16[384,4096]{1,0:T(8,128)(2,1)} async-done(((bf16[48,4096]{1,0:T(8,128)(2,1)}), bf16[384,4096]{1,0:T(8,128)(2,1)}) %all-gather.5.cloned.1.call-update) | async-done | bytes 3145744 | tf_op jit(solution)/shard_map/all_gather | solution.py:69
  99.0 5.0 %convolution_convert_fusion.4 = bf16[384,512]{1,0:T(8,128)(2,1)S(1)} fusion(bf16[384,4096]{1,0:T(8,128)(2,1)} %all-gather.5.cloned.1.call-done, bf16[512,4096]{1,0:T(8,128)(2,1)} %param.16), kind=kOutput, calls=%fused_computation.35 | convolution fusion | flops 1610809344 | bytes 7733248 | tf_op jit(solution)/shard_map/td,hd->th/dot_general | solution.py:67
  103.9 0.1 reshape.90
  104.0 118.5 %all-to-all-done = bf16[32,128,1024]{2,1,0:T(8,128)(2,1)} async-done(((bf16[32,128,1024]{2,1,0:T(8,128)(2,1)}), bf16[32,128,1024]{2,1,0:T(8,128)(2,1)}, u32[]{:S(2)}, u32[]{:S(2)}) %all-to-all-start) | async-done | bytes 8388640 | tf_op jit(solution)/shard_map/all_to_all | solution.py:40
  222.5 6.0 %gather_fusion.1 = bf16[12,128,1024]{2,1,0:T(8,128)(2,1)} fusion(bf16[32,128,1024]{2,1,0:T(8,128)(2,1)} %all-to-all-done, s32[1024]{0:T(1024)S(1)} %pad_clamp_fusion), kind=kCustom, calls=%fused_computation.1 | custom fusion | bytes 6291504 | tf_op jit(solution)/shard_map/gather | solution.py:41
  228.5 4.0 convolution_convert_fusion.1
  232.5 2.0 reshape.86
  234.5 5.2 %convolution_convert_fusion = bf16[1536,512]{1,0:T(8,128)(2,1)} fusion(bf16[1536,1024]{1,0:T(8,128)(2,1)} %bitcast.66, bf16[1024,512]{1,0:T(8,128)(2,1)} %param.14), kind=kOutput, calls=%fused_computation.9 | convolution fusion | flops 1611399168 | bytes 5767168 | tf_op jit(solution)/shard_map/dot_general | solution.py:43
  239.7 2.4 reshape.88
  242.0 0.7 convolution_multiply_fusion
  242.7 1.5 fusion.64
  244.2 0.2 copy-done.4
  244.4 0.8 copy-done.3
  245.3 1.8 fusion.21
  247.1 6.1 %fusion.19 = bf16[6,256,4,128]{1,3,2,0:T(8,128)(2,1)} fusion(bf16[6,64,4,128]{3,2,1,0:T(4,128)(2,1)S(1)} %reshape.90, f32[6,4,64]{2,1,0:T(4,128)S(1)} %get-tuple-element.3, f32[6,4,64,256]{3,2,1,0:T(8,128)} %copy-done.4), kind=kOutput, calls=%fused_computation.24 | convolution fusion | flops 102631168 | bytes 3545088 | tf_op jit(solution)/shard_map/chqk,cqhe->ckhe/dot_general | solution.py:87
  253.2 12.6 %fusion.16 = bf16[6,256,4,128]{1,3,2,0:T(8,128)(2,1)} fusion(f32[6,4,64,256]{3,2,1,0:T(8,128)} %fusion.21, bf16[6,64,4,128]{3,2,1,0:T(4,128)(2,1)S(1)} %reshape.87, f32[6,4,64,256]{3,2,1,0:T(8,128)} %get-tuple-element.4, f32[6,4,64]{2,1,0:T(4,128)S(1)} %get-tuple-element.3), kind=kOutput, calls=%fused_computation.23 | convolution fusion | flops 104204032 | bytes 5117952 | tf_op jit(solution)/shard_map/chqk,cqhe->ckhe/dot_general | solution.py:83
  265.8 3.9 copy.44
  269.7 5.9 %fusion.5 = f32[1536,1024]{1,0:T(8,128)} fusion(bf16[1024,512]{1,0:T(8,128)(2,1)S(1)} %copy-done.7, bf16[192,8,4,128]{3,2,1,0:T(4,128)(2,1)} %bitcast.68), kind=kOutput, calls=%fused_computation.16 | convolution fusion | flops 1610612736 | bytes 8912896 | tf_op jit(solution)/shard_map/td,ed->te/dot_general | solution.py:98
  275.6 3.8 copy.46
  279.5 6.8 %add_convert_fusion = bf16[1536,1024]{1,0:T(8,128)(2,1)} fusion(f32[1536,1024]{1,0:T(8,128)} %fusion.5, bf16[1024,512]{1,0:T(8,128)(2,1)S(1)} %copy-done.5, bf16[192,8,4,128]{3,2,1,0:T(4,128)(2,1)} %bitcast.64), kind=kOutput, calls=%fused_computation.7 | convolution fusion | flops 1613758464 | bytes 12058624 | tf_op jit(solution)/shard_map/td,ed->te/dot_general | solution.py:99
  286.3 6.8 %copy.47 = bf16[12,128,1024]{1,0,2:T(8,128)(2,1)} copy(bf16[12,128,1024]{2,1,0:T(8,128)(2,1)} %bitcast.63) | data formatting | bytes 6291456
  293.0 5.4 %copy.96 = bf16[128,8,12,128]{3,1,2,0:T(8,128)(2,1)} copy(bf16[128,8,12,128]{3,2,1,0:T(8,128)(2,1)} %bitcast.61) | data formatting | bytes 6291456
  298.5 0.0 reduce-scatter.10.cloned.1.call-update
  298.5 0.0 reduce-scatter.6.cloned.1.call-start
  298.6 5.1 %fusion.40 = bf16[6,64,4,128]{3,1,2,0:T(8,128)(2,1)S(1)} fusion(bf16[6,256,4,128]{3,2,1,0:T(4,128)(2,1)} %reshape.86, f32[6,4,64]{2,1,0:T(4,128)S(1)} %get-tuple-element.3, f32[6,4,64,256]{3,2,1,0:T(8,128)} %copy-done.4), kind=kOutput, calls=%fused_computation.38 | convolution fusion | flops 102041344 | bytes 3545088 | tf_op jit(solution)/shard_map/chqk,ckhe->cqhe/dot_general | solution.py:56
  303.7 0.3 copy.38
  304.0 6.6 %fusion.48 = f32[384,4096]{1,0:T(8,128)} fusion(bf16[512,4096]{1,0:T(8,128)(2,1)} %param.16, bf16[48,8,4,128]{3,2,1,0:T(4,128)(2,1)S(1)} %bitcast.69), kind=kOutput, calls=%fused_computation.45 | convolution fusion | flops 1610612736 | bytes 10878976 | tf_op jit(solution)/shard_map/dot_general | solution.py:62
  310.6 0.0 reduce-scatter.6.cloned.1.call-update
  310.7 0.0 reduce-scatter.8.cloned.1.call-start
  310.7 11.1 %fusion.35 = bf16[6,64,4,128]{3,1,2,0:T(8,128)(2,1)S(1)} fusion(bf16[6,256,4,128]{3,2,1,0:T(4,128)(2,1)S(1)} %reshape.88, f32[6,4,64,256]{3,2,1,0:T(8,128)} %fusion.21, f32[6,4,64,256]{3,2,1,0:T(8,128)} %get-tuple-element.4, f32[6,4,64]{2,1,0:T(4,128)S(1)} %get-tuple-element.3), kind=kOutput, calls=%fused_computation.37 | convolution fusion | flops 103614208 | bytes 5117952 | tf_op jit(solution)/shard_map/chqk,ckhe->cqhe/dot_general | solution.py:79
  321.9 0.3 copy.42
  322.2 6.8 %fusion.45 = f32[384,4096]{1,0:T(8,128)} fusion(bf16[4096,512]{1,0:T(8,128)(2,1)} %param.13, bf16[48,8,4,128]{3,2,1,0:T(4,128)(2,1)S(1)} %bitcast.70), kind=kOutput, calls=%fused_computation.42 | convolution fusion | flops 1610612736 | bytes 10878976 | tf_op jit(solution)/shard_map/td,ed->te/dot_general | solution.py:93
  328.9 0.0 reduce-scatter.8.cloned.1.call-update
  329.0 13.1 %reduce-scatter.10.cloned.1.call-done = bf16[128,1536]{1,0:T(8,128)(2,1)} async-done(((bf16[1024,1536]{1,0:T(8,128)(2,1)}), bf16[128,1536]{1,0:T(8,128)(2,1)}) %reduce-scatter.10.cloned.1.call-update) | async-done | bytes 393232
  342.0 1.3 reshape.127
  343.3 0.4 copy.48
  343.7 0.1 convert_element_type.81
  343.8 0.2 broadcast_in_dim.34
  344.0 1.0 scatter_fusion
  345.0 0.2 convert_element_type.82
  345.2 35.0 %all_to_all.10 = bf16[32,128,128]{2,1,0:T(8,128)(2,1)S(1)} all-to-all(bf16[32,128,128]{2,1,0:T(8,128)(2,1)S(1)} %convert_element_type.82), channel_id=1, replica_groups=mesh['dp'=32,'mp'=8] {'dp'}, dimensions={0} | all-to-all | bytes 2097152 | tf_op jit(solution)/shard_map/all_to_all | solution.py:107
  380.2 0.2 convert_element_type.83
  380.5 2.7 scatter_fusion.1
  383.2 0.0 copy-start.2
  383.2 5.2 %reduce-scatter.6.cloned.1.call-done = f32[48,4096]{1,0:T(8,128)} async-done(((f32[384,4096]{1,0:T(8,128)}), f32[48,4096]{1,0:T(8,128)}) %reduce-scatter.6.cloned.1.call-update) | async-done | bytes 786448 | tf_op jit(solution)/shard_map/reduce_scatter | solution.py:61
  388.4 1.9 convert_element_type.69
  390.3 45.2 %reduce-scatter.8.cloned.1.call-done = f32[48,4096]{1,0:T(8,128)} async-done(((f32[384,4096]{1,0:T(8,128)}), f32[48,4096]{1,0:T(8,128)}) %reduce-scatter.8.cloned.1.call-update) | async-done | bytes 786448 | tf_op jit(solution)/shard_map/reduce_scatter | solution.py:92
  435.6 1.9 convert_element_type.74
  (18 shorter events, 0.1 us)
Async XLA Ops:
  7.2 1.6 copy-start
  20.8 13.5 %copy-start.6 = (s32[32,6,2]{0,2,1:T(2,128)S(1)}, s32[32,6,2]{0,2,1:T(2,128)}, u32[]{:S(2)}) copy-start(s32[32,6,2]{0,2,1:T(2,128)} %param.11) | copy-start | bytes 4612
  20.8 201.7 %all-to-all-start = ((bf16[32,128,1024]{2,1,0:T(8,128)(2,1)}), bf16[32,128,1024]{2,1,0:T(8,128)(2,1)}, u32[]{:S(2)}, u32[]{:S(2)}) async-start(bf16[32,128,1024]{2,1,0:T(8,128)(2,1)} %broadcast_select_fusion), calls=%async_computation | async-start | bytes 16777216 | tf_op jit(solution)/shard_map/all_to_all | solution.py:40
  32.8 33.9 %all-gather.3.cloned.1.call-start = ((), (), s32[]{:S(2)}) async-start(), calls=%async_computation.5 | async-start | bytes 3538944 | tf_op jit(solution)/shard_map/all_gather | solution.py:35
  33.5 65.4 %all-gather.5.cloned.1.call-start = ((), (), s32[]{:S(2)}) async-start(), calls=%async_computation.7 | async-start | bytes 3538944 | tf_op jit(solution)/shard_map/all_gather | solution.py:69
  34.3 307.7 %reduce-scatter.10.cloned.1.call-start = ((), (), s32[]{:S(2)}) async-start(), calls=%async_computation.9 | async-start | bytes 3538944
  242.7 1.7 copy-start.4
  242.7 2.5 copy-start.3
  265.8 3.9 copy-start.7
  275.6 3.8 copy-start.5
  298.5 89.9 %reduce-scatter.6.cloned.1.call-start = ((), (), s32[]{:S(2)}) async-start(), calls=%async_computation.6 | async-start | bytes 7077888 | tf_op jit(solution)/shard_map/reduce_scatter | solution.py:61
  310.7 124.9 %reduce-scatter.8.cloned.1.call-start = ((), (), s32[]{:S(2)}) async-start(), calls=%async_computation.8 | async-start | bytes 7077888 | tf_op jit(solution)/shard_map/reduce_scatter | solution.py:92
  380.5 57.0 %copy-start.1 = (bf16[4,128,1024]{2,1,0:T(8,128)(2,1)S(1)}, bf16[4,128,1024]{2,1,0:T(8,128)(2,1)}, u32[]{:S(2)}) copy-start(bf16[4,128,1024]{2,1,0:T(8,128)(2,1)} %param.10) | copy-start | bytes 3145732
  383.2 54.3 %copy-start.2 = (f32[4,128,128]{2,1,0:T(8,128)}, f32[4,128,128]{2,1,0:T(8,128)S(1)}, u32[]{:S(2)}) copy-start(f32[4,128,128]{2,1,0:T(8,128)S(1)} %scatter_fusion.1) | copy-start | bytes 786436
Sparse Core Ops, SparseCore 0:
  35.5 31.2 all-gather.2
  68.6 30.3 all-gather.4
  298.6 43.3 reduce-scatter.9
  344.4 43.9 reduce-scatter.5
  390.8 44.7 reduce-scatter.7
where the time goes:
time: 445 us; the launch traced here: 444 us
  waiting for transfers between devices  243 us (55%)
  matrix products  82.6 us (19%)
  local copies, waits for them, and re-layouts  40.2 us (9%)
  blocking collectives  35 us (8%)
  other arithmetic  17.2 us (4%)
  between operations  14 us (3%)
  starting transfers between devices  12.2 us (3%)
    all_to_all x1, waiting for transfers between devices, body(): lax.all_to_all(outgoing, 'dp', split_axis=0, concat_axis=0, tiled=True)  119 us
    reduce_scatter x1, waiting for transfers between devices, body(): lax.psum_scatter(jnp.einsum('td,ed->te', picked, w_query, preferred_eleme...  45.2 us
    all_to_all x1, blocking collectives, body(): lax.all_to_all(returning.astype(jnp.bfloat16), 'dp', split_axis=0, concat...  35 us
    all_gather x1, waiting for transfers between devices, body(): lax.all_gather(tokens, 'mp', axis=0, tiled=True)  32.2 us
    all_gather x1, waiting for transfers between devices, body(): lax.all_gather(grad_out, 'mp', axis=0, tiled=True)  27.2 us
    unnamed x21, local copies, waits for them, and re-layouts  15.1 us
    unnamed x6, waiting for transfers between devices  14.5 us
    dot_general x1, matrix products, body(): jnp.einsum('chqk,cqhe->ckhe', grad_scores, query_blocks, preferred_elemen...  12.6 us
  transfers between devices with their start and end apart: 6, of which 6 were waited for; matrix products, arithmetic and copies ran while one was open for 11% of the time, Pallas kernels for 0%

commit v1 on v0

v1 whole, which is shorter than its diff:
```python
import functools
import math

import jax
import jax.numpy as jnp
from jax import lax
from jax.experimental import pallas as pl
from jax.experimental.pallas import tpu as pltpu
from jax.sharding import PartitionSpec as P

HD = 128
GROUP = 64
NBR = 2
XS = 4
CORES = 2
BF = jnp.bfloat16
F32 = jnp.float32
NT = (((1,), (1,)), ((), ()))
TN = (((0,), (0,)), ((), ()))


def mm(a, b):
    return jnp.dot(a, b, preferred_element_type=F32)


def mm_nt(a, b):
    return lax.dot_general(a, b, NT, preferred_element_type=F32)


def mm_tn(a, b):
    return lax.dot_general(a, b, TN, preferred_element_type=F32)


def x_perm(step):
    return [(2 * x + c, 2 * ((x + step) % XS) + c) for x in range(XS) for c in range(CORES)]


CORE_SWAP = [(2 * x + c, 2 * x + 1 - c) for x in range(XS) for c in range(CORES)]


def gather_pieces(block):
    own = [block]
    for step in (1, -1, 2):
        own.append(lax.ppermute(block, "mp", x_perm(step)))
    other = [lax.ppermute(piece, "mp", CORE_SWAP) for piece in own]
    return own + other


def piece_owners(x, c):
    own = [2 * ((x + XS - step) % XS) + c for step in (0, 1, -1, 2)]
    other = [2 * ((x + XS - step) % XS) + 1 - c for step in (0, 1, -1, 2)]
    return jnp.stack(own + other).astype(jnp.int32)


def project_kernel(owner_ref, *refs):
    t_refs, g_refs = refs[:8], refs[8:16]
    wq_ref, wo_ref, q_ref, gh_ref, q_acc, gh_acc = refs[16:]
    step = pl.program_id(0)
    t = jnp.concatenate([r[...] for r in t_refs], axis=0)
    g = jnp.concatenate([r[...] for r in g_refs], axis=0)
    dq = mm(t, wq_ref[...])
    dg = mm_nt(g, wo_ref[...])

    @pl.when(step == 0)
    def _():
        q_acc[...] = dq
        gh_acc[...] = dg

    @pl.when(step > 0)
    def _():
        q_acc[...] += dq
        gh_acc[...] += dg

    @pl.when(step == pl.num_programs(0) - 1)
    def _():
        rows = t_refs[0].shape[0]
        for j in range(8):
            at = pl.ds(pl.multiple_of(owner_ref[j] * rows, rows), rows)
            q_ref[at, :] = q_acc[j * rows : (j + 1) * rows, :].astype(BF)
            gh_ref[at, :] = gh_acc[j * rows : (j + 1) * rows, :].astype(BF)


def project(owners, t_pieces, g_pieces, w_query, w_out):
    rows, depth = t_pieces[0].shape
    width = w_query.shape[1]
    cut = 512
    piece = pl.BlockSpec((rows, cut), lambda i, s: (0, i))
    whole = pl.BlockSpec((8 * rows, width), lambda i, s: (0, 0))
    out = jax.ShapeDtypeStruct((8 * rows, width), BF)
    return pl.pallas_call(
        project_kernel,
        grid_spec=pltpu.PrefetchScalarGridSpec(
            num_scalar_prefetch=1,
            grid=(depth // cut,),
            in_specs=[piece] * 16
            + [
                pl.BlockSpec((cut, width), lambda i, s: (i, 0)),
                pl.BlockSpec((width, cut), lambda i, s: (0, i)),
            ],
            out_specs=[whole, whole],
            scratch_shapes=[pltpu.VMEM((8 * rows, width), F32)] * 2,
        ),
        out_shape=[out, out],
        compiler_params=pltpu.CompilerParams(vmem_limit_bytes=24 << 20),
        cost_estimate=pl.CostEstimate(
            flops=4 * 8 * rows * depth * width, bytes_accessed=15 << 20, transcendentals=0
        ),
        name="project",
    )(owners, *t_pieces, *g_pieces, w_query, w_out)


def attend_kernel(owner_ref, *refs):
    p_refs = refs[:8]
    q_ref, gh_ref, wk_ref, wv_ref, ho_ref, gq_ref, keep_ref, send_ref, near, grad = refs[8:]
    heads = q_ref.shape[1] // HD
    scale = 1.0 / math.sqrt(HD)
    keys = near.shape[0]
    for j in range(8):
        at = pl.ds(pl.multiple_of(owner_ref[j] * 128, 128), 128)
        near[:, at] = p_refs[j][...].reshape(keys, 128)
    rows = near[...]
    k = mm(rows, wk_ref[...]).astype(BF)
    v = mm(rows, wv_ref[...]).astype(BF)
    q = q_ref[...]
    gh = gh_ref[...]
    part = [slice(h * HD, (h + 1) * HD) for h in range(heads)]
    s = jnp.concatenate([mm_nt(q[:, p], k[:, p]) for p in part], axis=0) * scale
    gp = jnp.concatenate([mm_nt(gh[:, p], v[:, p]) for p in part], axis=0)
    e = jnp.exp(s - jnp.max(s, axis=-1, keepdims=True))
    probs = e * (1.0 / jnp.sum(e, axis=-1, keepdims=True))
    pb = probs.astype(BF)
    centre = jnp.sum(probs * gp, axis=-1, keepdims=True)
    gs = (probs * (gp - centre) * scale).astype(BF)
    gk = []
    gv = []
    for h, p in enumerate(part):
        r = slice(h * GROUP, (h + 1) * GROUP)
        ho_ref[:, p] = mm(pb[r], v[:, p]).astype(BF)
        gq_ref[:, p] = mm(gs[r], k[:, p]).astype(BF)
        gk.append(mm_tn(gs[r], q[:, p]).astype(BF))
        gv.append(mm_tn(pb[r], gh[:, p]).astype(BF))
    gk = jnp.concatenate(gk, axis=1)
    gv = jnp.concatenate(gv, axis=1)
    grad[...] = mm_nt(gk, wk_ref[...]) + mm_nt(gv, wv_ref[...])
    for step in range(XS):
        mine = pl.ds(pl.multiple_of(owner_ref[8 + step] * 128, 128), 128)
        keep_ref[step] = grad[:, mine].astype(BF).reshape(keep_ref.shape[1:])
        sibling = pl.ds(pl.multiple_of(owner_ref[8 + XS + step] * 128, 128), 128)
        send_ref[step] = grad[:, sibling].astype(BF).reshape(send_ref.shape[1:])


def attend(indices, pieces, q, gh, w_key, w_value):
    neigh, depth, cols = pieces[0].shape
    length, width = q.shape
    groups = length // GROUP
    piece = pl.BlockSpec((NBR, depth, cols), lambda i, s: (i, 0, 0))
    rows = pl.BlockSpec((GROUP, width), lambda i, s: (i, 0))
    weight = pl.BlockSpec(w_key.shape, lambda i, s: (0, 0), pipeline_mode=pl.Buffered(1))
    share = pl.BlockSpec((XS, NBR, depth, cols), lambda i, s: (0, i, 0, 0))
    small = jax.ShapeDtypeStruct((length, width), BF)
    half = jax.ShapeDtypeStruct((XS, neigh, depth, cols), BF)
    return pl.pallas_call(
        attend_kernel,
        grid_spec=pltpu.PrefetchScalarGridSpec(
            num_scalar_prefetch=1,
            grid=(groups,),
            in_specs=[piece] * 8 + [rows, rows, weight, weight],
            out_specs=[rows, rows, share, share],
            scratch_shapes=[
                pltpu.VMEM((NBR * depth, 8 * cols), BF),
                pltpu.VMEM((NBR * depth, 8 * cols), F32),
            ],
        ),
        out_shape=[small, small, half, half],
        compiler_params=pltpu.CompilerParams(vmem_limit_bytes=32 << 20),
        cost_estimate=pl.CostEstimate(
            flops=8 * neigh * depth * 8 * cols * width,
            bytes_accessed=12 << 20,
            transcendentals=length * 4 * NBR * depth,
        ),
        name="attend",
    )(indices, *pieces, q, gh, w_key, w_value)


def out_kernel(index_ref, a_ref, w_ref, keep_ref, send_ref, *, transposed):
    rows = keep_ref.shape[1]
    blocks = []
    for j in range(8):
        at = pl.ds(pl.multiple_of(index_ref[8 + j] * rows, rows), rows)
        blocks.append(a_ref[at, :])
    a = jnp.concatenate(blocks, axis=0)
    r = (mm_nt if transposed else mm)(a, w_ref[...]).astype(BF)
    keep_ref[...] = r[: XS * rows].reshape(keep_ref.shape)
    send_ref[...] = r[XS * rows :].reshape(send_ref.shape)


def out_project(indices, a, w, transposed, name):
    length, width = a.shape
    full = w.shape[0] if transposed else w.shape[1]
    rows = length // 8
    cut = 1024
    if transposed:
        weight = pl.BlockSpec((cut, width), lambda i, s: (i, 0))
    else:
        weight = pl.BlockSpec((width, cut), lambda i, s: (0, i))
    half_spec = pl.BlockSpec((XS, rows, cut), lambda i, s: (0, 0, i))
    half = jax.ShapeDtypeStruct((XS, rows, full), BF)
    return pl.pallas_call(
        functools.partial(out_kernel, transposed=transposed),
        grid_spec=pltpu.PrefetchScalarGridSpec(
            num_scalar_prefetch=1,
            grid=(full // cut,),
            in_specs=[pl.BlockSpec((length, width), lambda i, s: (0, 0)), weight],
            out_specs=[half_spec, half_spec],
        ),
        out_shape=[half, half],
        compiler_params=pltpu.CompilerParams(vmem_limit_bytes=24 << 20),
        cost_estimate=pl.CostEstimate(
            flops=2 * length * width * full, bytes_accessed=8 << 20, transcendentals=0
        ),
        name=name,
    )(indices, a, w)


def chip_sums(keep, send):
    got = lax.ppermute(send, "mp", CORE_SWAP)
    return [(keep[i].astype(F32) + got[i].astype(F32)).astype(BF) for i in range(XS)]


def x_sum(sums):
    total = sums[0].astype(F32)
    for step in range(1, XS):
        total = total + lax.ppermute(sums[step], "mp", x_perm(step)).astype(F32)
    return total.astype(BF)


def body(
    tokens, encoded, neighbour_owner, neighbour_slot, w_query, w_key, w_value, w_out, grad_out
):
    dp_count = lax.axis_size("dp")
    dp_at = lax.axis_index("dp")
    mp_at = lax.axis_index("mp")
    x, c = mp_at // CORES, mp_at % CORES
    neigh = neighbour_owner.shape[1] * NBR
    share = encoded.shape[2] // (XS * CORES)
    owners = piece_owners(x, c)
    targets = jnp.stack(
        [2 * ((x + i) % XS) + c for i in range(XS)]
        + [2 * ((x + i) % XS) + 1 - c for i in range(XS)]
    ).astype(jnp.int32)
    indices = jnp.concatenate([owners, targets])

    owners_all = neighbour_owner.reshape(dp_count, neigh)
    slots_all = neighbour_slot.reshape(dp_count, neigh)
    held_here = owners_all == dp_at
    wanted = jnp.any(held_here, axis=1)
    held_slot = jnp.sum(jnp.where(held_here, slots_all, 0), axis=1)
    my_owners = lax.dynamic_index_in_dim(owners_all, dp_at, 0, keepdims=False)
    place = jnp.argmax(my_owners[None, :] == jnp.arange(dp_count)[:, None], axis=1)

    t_pieces = gather_pieces(tokens)
    g_pieces = gather_pieces(grad_out)

    mine = lax.dynamic_slice_in_dim(encoded, mp_at * share, share, axis=2)
    arrived = lax.all_to_all(mine[held_slot], "dp", split_axis=0, concat_axis=0, tiled=True)
    n_pieces = gather_pieces(arrived[my_owners])

    query, grad_heads = project(owners, t_pieces, g_pieces, w_query, w_out)
    heads_out, grad_query, n_keep, n_send = attend(
        indices, n_pieces, query, grad_heads, w_key, w_value
    )
    grad_share = x_sum(chip_sums(n_keep, n_send))
    returned = lax.all_to_all(grad_share[place], "dp", split_axis=0, concat_axis=0, tiled=True)

    attended = x_sum(chip_sums(*out_project(indices, heads_out, w_out, False, "attended")))
    grad_tokens = x_sum(chip_sums(*out_project(indices, grad_query, w_query, True, "gtokens")))

    pick = (held_slot[None, :] == jnp.arange(encoded.shape[0])[:, None]) & wanted[None, :]
    grad_encoded = jnp.dot(
        pick.astype(BF), returned.reshape(dp_count, -1), preferred_element_type=F32
    ).reshape(encoded.shape[0], encoded.shape[1], share)
    return (attended, grad_tokens, grad_encoded)


def solution(mesh):
    placed = (
        P(("dp", "mp"), None),
        P("dp", None, None),
        P(),
        P(),
        P(None, "mp"),
        P(None, "mp"),
        P(None, "mp"),
        P("mp", None),
        P(("dp", "mp"), None),
    )
    return jax.shard_map(
        body,
        mesh=mesh,
        in_specs=placed,
        out_specs=(P(("dp", "mp"), None), P(("dp", "mp"), None), P("dp", None, "mp")),
        check_vma=False,
    )
```

time: 445 us -> 185 us (0.42)
  waiting for transfers between devices: 243 us -> 72 us
  matrix products: 82.6 us -> 1.89 us
  starting transfers between devices: 12.2 us -> 52.1 us
  blocking collectives: 35 us -> 0 us
  Pallas kernels: 0 us -> 32.2 us
  local copies, waits for them, and re-layouts: 40.2 us -> 14.2 us
  between operations: 14 us -> 0.92 us
  other arithmetic: 17.2 us -> 10 us
    all_to_all x1 -> x2, waiting for transfers between devices: 119 us -> 2.28 us  [the longest x1 2.27 us: body(): lax.all_to_all(grad_share[place], 'dp', split_axis=0, concat_axis=0, tile...]
    dot_general x14 -> x1, matrix products: 82.6 us -> 1.89 us  [body(): jnp.dot(pick.astype(BF), returned.reshape(dp_count, -1), preferred_elemen...]
    ppermute x0 -> x33, waiting for transfers between devices: none -> 69.7 us  [the longest x9 42.4 us: gather_pieces(): own.append(lax.ppermute(block, 'mp', x_perm(step)))]
    all_gather x2 -> x0, waiting for transfers between devices: 59.4 us -> none  [the longest x1 32.2 us: body(): lax.all_gather(tokens, 'mp', axis=0, tiled=True)]
    reduce_scatter x2 -> x0, waiting for transfers between devices: 50.4 us -> none  [the longest x1 45.2 us: body(): lax.psum_scatter(jnp.einsum('td,ed->te', picked, w_query, preferred_eleme...]
    all_to_all x1 -> x0, blocking collectives: 35 us -> none  [body(): lax.all_to_all(returning.astype(jnp.bfloat16), 'dp', split_axis=0, concat...]
    pallas_call x0 -> x4, Pallas kernels: none -> 32.2 us  [the longest x1 16.4 us: attend(): pl.pallas_call(attend_kernel, grid_spec=pltpu.PrefetchScalarGridSpec(num_...]
    ppermute x0 -> x33, starting transfers between devices: none -> 30.4 us  [the longest x9 15.1 us: gather_pieces(): own.append(lax.ppermute(block, 'mp', x_perm(step)))]
  transfers between devices with their start and end apart: 6 -> 35, of which waited for: 6 -> 12; matrix products, arithmetic and copies ran while one was open for 11% -> 7% of each run, Pallas kernels for 0% -> 9%
where the time goes in v1:
time: 185 us; the launch traced here: 183 us
  waiting for transfers between devices  72 us (39%)
  starting transfers between devices  52.1 us (28%)
  Pallas kernels  32.2 us (17%)
  local copies, waits for them, and re-layouts  14.2 us (8%)
  other arithmetic  10 us (5%)
  matrix products  1.89 us (1%)
    ppermute x9, waiting for transfers between devices, gather_pieces(): own.append(lax.ppermute(block, 'mp', x_perm(step)))  42.4 us
    ppermute x9, waiting for transfers between devices, x_sum(): total = total + lax.ppermute(sums[step], 'mp', x_perm(step)).astype(F32)  27.2 us
    pallas_call x1, Pallas kernels, attend(): pl.pallas_call(attend_kernel, grid_spec=pltpu.PrefetchScalarGridSpec(num_...  16.4 us
    ppermute x9, starting transfers between devices, gather_pieces(): own.append(lax.ppermute(block, 'mp', x_perm(step)))  15.1 us
    ppermute x9, starting transfers between devices, x_sum(): total = total + lax.ppermute(sums[step], 'mp', x_perm(step)).astype(F32)  12.4 us
    all_to_all x1, starting transfers between devices, body(): lax.all_to_all(mine[held_slot], 'dp', split_axis=0, concat_axis=0, tiled=...  11.9 us
    all_to_all x1, starting transfers between devices, body(): lax.all_to_all(grad_share[place], 'dp', split_axis=0, concat_axis=0, tile...  9.83 us
    unnamed x34, local copies, waits for them, and re-layouts  8.63 us
  transfers between devices with their start and end apart: 35, of which 12 were waited for; matrix products, arithmetic and copies ran while one was open for 7% of the time, Pallas kernels for 9%

profile of v1, /device:TPU:8, one launch (start us, length us, event | category | flops | bytes accessed | tf_op | source)
XLA Modules:
  0.0 183.2 jit_solution(6131916390023710925)
XLA Ops:
  0.7 0.8 select_reduce_fusion
  1.5 0.4 copy-done
  1.9 1.7 gather_fusion
  3.6 11.9 %all-to-all-start = ((bf16[32,128,128]{2,1,0:T(8,128)(2,1)}), bf16[32,128,128]{2,1,0:T(8,128)(2,1)}, u32[]{:S(2)}, u32[]{:S(2)}) async-start(bf16[32,128,128]{2,1,0:T(8,128)(2,1)} %gather_fusion), calls=%async_computation | async-start | bytes 2097152 | tf_op jit(solution)/shard_map/all_to_all | solution.py:265
  15.5 1.6 collective-permute-start.7
  17.1 1.7 collective-permute-start.8
  18.8 1.8 collective-permute-start.9
  20.6 0.6 collective-permute-start.14
  21.2 2.6 %collective-permute-start.15 = (bf16[48,4096]{1,0:T(8,128)(2,1)S(1)}, bf16[48,4096]{1,0:T(8,128)(2,1)S(1)}, u32[]{:S(2)}, u32[]{:S(2)}) collective-permute-start(bf16[48,4096]{1,0:T(8,128)(2,1)S(1)} %copy-done.7), channel_id=1, source_target_pairs={{0,6},{1,7},{2,0},{3,1},{4,2},{5,3},{6,4},{7,5},{8,14},{9,15},{10,... | collective-permute-start | bytes 1179656 | tf_op jit(solution)/shard_map/ppermute | solution.py:44
  23.9 12.4 %collective-permute-done.7.refs_1_ = bf16[48,4096]{1,0:T(8,128)(2,1)S(1)} collective-permute-done((bf16[48,4096]{1,0:T(8,128)(2,1)S(1)}, bf16[48,4096]{1,0:T(8,128)(2,1)S(1)}, u32[]{:S(2)}, u32[]{:S(2)}) %collective-permute-start.7) | collective-permute-done | bytes 393248 | tf_op jit(solution)/shard_map/ppermute | solution.py:44
  36.2 2.8 %collective-permute-start.16 = (bf16[48,4096]{1,0:T(8,128)(2,1)S(1)}, bf16[48,4096]{1,0:T(8,128)(2,1)}, u32[]{:S(2)}, u32[]{:S(2)}) collective-permute-start(bf16[48,4096]{1,0:T(8,128)(2,1)S(1)} %copy-done.7), channel_id=1, source_target_pairs={{0,4},{1,5},{2,6},{3,7},{4,0},{5,1},{6,2},{7,3},{8,12},{9,13},{10,... | collective-permute-start | bytes 1179656 | tf_op jit(solution)/shard_map/ppermute | solution.py:44
  39.1 0.6 collective-permute-start.17
  39.7 5.1 %collective-permute-done.14.refs_9_ = bf16[48,4096]{1,0:T(8,128)(2,1)} collective-permute-done((bf16[48,4096]{1,0:T(8,128)(2,1)S(1)}, bf16[48,4096]{1,0:T(8,128)(2,1)}, u32[]{:S(2)}, u32[]{:S(2)}) %collective-permute-start.14) | collective-permute-done | bytes 393248 | tf_op jit(solution)/shard_map/ppermute | solution.py:44
  44.8 1.2 collective-permute-done.15.refs_10_
  46.0 7.5 %collective-permute-done.16.refs_11_ = bf16[48,4096]{1,0:T(8,128)(2,1)} collective-permute-done((bf16[48,4096]{1,0:T(8,128)(2,1)S(1)}, bf16[48,4096]{1,0:T(8,128)(2,1)}, u32[]{:S(2)}, u32[]{:S(2)}) %collective-permute-start.16) | collective-permute-done | bytes 393248 | tf_op jit(solution)/shard_map/ppermute | solution.py:44
  53.6 0.1 copy.20
  53.7 0.5 collective-permute-start.18
  54.2 1.8 %gather_fusion.1 = bf16[12,128,128]{2,1,0:T(8,128)(2,1)S(1)} fusion(bf16[32,128,128]{2,1,0:T(8,128)(2,1)} %all-to-all-done, s32[1024]{0:T(1024)S(1)} %pad_clamp_fusion.1), kind=kCustom, calls=%fused_computation.1 | custom fusion | bytes 786480 | tf_op jit(solution)/shard_map/gather | solution.py:266
  56.1 0.1 collective-permute-start.19
  56.2 1.2 collective-permute-start
  57.4 2.1 %collective-permute-start.1 = (bf16[12,128,128]{2,1,0:T(8,128)(2,1)S(1)}, bf16[12,128,128]{2,1,0:T(8,128)(2,1)}, u32[]{:S(2)}, u32[]{:S(2)}) collective-permute-start(bf16[12,128,128]{2,1,0:T(8,128)(2,1)S(1)} %gather_fusion.1), channel_id=1, source_target_pairs={{0,6},{1,7},{2,0},{3,1},{4,2},{5,3},{6,4},{7,5},{8,14},{9,15},{10,... | collective-permute-start | bytes 1179656 | tf_op jit(solution)/shard_map/ppermute | solution.py:44
  59.5 0.6 collective-permute-start.2
  60.1 0.7 copy-done.10
  60.8 0.5 collective-permute-start.3
  61.3 8.4 %collective-permute-done.refs_1_ = bf16[12,128,128]{2,1,0:T(8,128)(2,1)} collective-permute-done((bf16[12,128,128]{2,1,0:T(8,128)(2,1)S(1)}, bf16[12,128,128]{2,1,0:T(8,128)(2,1)}, u32[]{:S(2)}, u32[]{:S(2)}) %collective-permute-start) | collective-permute-done | bytes 393248 | tf_op jit(solution)/shard_map/ppermute | solution.py:44
  69.8 6.9 %collective-permute-done.1.refs_2_ = bf16[12,128,128]{2,1,0:T(8,128)(2,1)} collective-permute-done((bf16[12,128,128]{2,1,0:T(8,128)(2,1)S(1)}, bf16[12,128,128]{2,1,0:T(8,128)(2,1)}, u32[]{:S(2)}, u32[]{:S(2)}) %collective-permute-start.1) | collective-permute-done | bytes 393248 | tf_op jit(solution)/shard_map/ppermute | solution.py:44
  76.7 0.9 collective-permute-done.2.refs_3_
  77.7 0.1 concatenate.4.owner_ref.index_ref
  77.8 2.2 %copy-done.1 = bf16[4096,512]{1,0:T(8,128)(2,1)S(1)} copy-done((bf16[4096,512]{1,0:T(8,128)(2,1)S(1)}, bf16[4096,512]{1,0:T(8,128)(2,1)}, u32[]{:S(2)}) %copy-start.1) | copy-done | bytes 4194328
  80.0 2.2 %copy-done.3 = bf16[512,4096]{1,0:T(8,128)(2,1)S(1)} copy-done((bf16[512,4096]{1,0:T(8,128)(2,1)S(1)}, bf16[512,4096]{1,0:T(8,128)(2,1)}, u32[]{:S(2)}) %copy-start.3) | copy-done | bytes 4194328
  82.2 1.0 copy-done.9
  83.2 1.0 copy-done.11
  84.2 8.5 %project.1 = (bf16[384,512]{1,0:T(8,128)(2,1)S(1)}, bf16[384,512]{1,0:T(8,128)(2,1)S(1)}) custom-call(s32[8]{0:T(128)S(1)} %stack.55.owner_ref, bf16[48,4096]{1,0:T(8,128)(2,1)S(1)} %copy-done.6, bf16[48,4096]{1,0:T(8,128)(2,1)S(1)} %collective-permute-done.7.refs_1_, bf16[48,4096]{1,0:T(8,128)(2,1)S(1)} %collective-permute-done.8.refs_2_, ...), custom_call_target="tpu_custom_call" | custom-call | flops 3221225472 | bytes 15728640 | tf_op jit(solution)/shard_map/project/pallas_call | solution.py:90
  92.8 16.4 %attend.1 = (bf16[384,512]{1,0:T(8,128)(2,1)S(1)}, bf16[384,512]{1,0:T(8,128)(2,1)S(1)}, bf16[4,12,128,128]{3,2,1,0:T(8,128)(2,1)S(1)}, bf16[4,12,128,128]{3,2,1,0:T(8,128)(2,1)S(1)}) custom-call(s32[16]{0:T(128)S(1)} %concatenate.4.owner_ref.index_ref, bf16[12,128,128]{2,1,0:T(8,128)(2,1)S(1)} %gather_fusion.1, ...), custom_call_target="tpu_custom_call" | custom-call | flops 6442450944 | bytes 12582912 | tf_op jit(solution)/shard_map/attend/pallas_call | solution.py:162
  109.2 0.6 collective-permute-start.29
  109.8 3.2 %gtokens.1 = (bf16[4,48,4096]{2,1,0:T(8,128)(2,1)S(1)}, bf16[4,48,4096]{2,1,0:T(8,128)(2,1)S(1)}) custom-call(s32[16]{0:T(128)S(1)} %concatenate.4.owner_ref.index_ref, bf16[384,512]{1,0:T(8,128)(2,1)S(1)} %get-tuple-element.19.a_ref, bf16[4096,512]{1,0:T(8,128)(2,1)S(1)} %copy-done.2), custom_call_target="tpu_custom_call" | custom-call | flops 1610612736 | bytes 8388608 | tf_op jit(solution)/shard_map/gtokens/pallas_call | solution.py:208
  113.0 0.1 collective-permute-start.25
  113.1 0.6 iota_reduce_fusion
  113.7 4.1 %attended.1 = (bf16[4,48,4096]{2,1,0:T(8,128)(2,1)S(1)}, bf16[4,48,4096]{2,1,0:T(8,128)(2,1)}) custom-call(s32[16]{0:T(128)S(1)} %concatenate.4.owner_ref.index_ref, bf16[384,512]{1,0:T(8,128)(2,1)S(1)} %get-tuple-element.16.a_ref, bf16[512,4096]{1,0:T(8,128)(2,1)S(1)} %copy-done.4), custom_call_target="tpu_custom_call" | custom-call | flops 1610612736 | bytes 8388608 | tf_op jit(solution)/shard_map/attended/pallas_call | solution.py:208
  117.8 0.5 collective-permute-start.21
  118.3 0.5 fusion.21
  118.8 0.1 copy-done.5
  119.0 1.1 collective-permute-start.30
  120.1 3.7 %collective-permute-start.31 = (bf16[12,128,128]{2,1,0:T(8,128)(2,1)S(1)}, bf16[12,128,128]{2,1,0:T(8,128)(2,1)S(1)}, u32[]{:S(2)}, u32[]{:S(2)}) collective-permute-start(bf16[12,128,128]{2,1,0:T(8,128)(2,1)S(1)} %get-tuple-element.36), channel_id=1, source_target_pairs={{0,4},{1,5},{2,6},{3,7},{4,0},{5,1},{6,2},{7,3},{8,12},{9,13},{10,... | collective-permute-start | bytes 1179656 | tf_op jit(solution)/shard_map/ppermute | solution.py:233
  123.8 1.5 fusion.17
  125.2 0.1 copy-done.14
  125.4 2.0 %collective-permute-start.26 = (bf16[48,4096]{1,0:T(8,128)(2,1)}, bf16[48,4096]{1,0:T(8,128)(2,1)S(1)}, u32[]{:S(2)}, u32[]{:S(2)}) collective-permute-start(bf16[48,4096]{1,0:T(8,128)(2,1)} %get-tuple-element.37), channel_id=1, source_target_pairs={{0,2},{1,3},{2,4},{3,5},{4,6},{5,7},{6,0},{7,1},{8,10},{9,11},{10,... | collective-permute-start | bytes 1179656 | tf_op jit(solution)/shard_map/ppermute | solution.py:233
  127.4 5.1 %collective-permute-done.30 = bf16[12,128,128]{2,1,0:T(8,128)(2,1)S(1)} collective-permute-done((bf16[12,128,128]{2,1,0:T(8,128)(2,1)S(1)}, bf16[12,128,128]{2,1,0:T(8,128)(2,1)S(1)}, u32[]{:S(2)}, u32[]{:S(2)}) %collective-permute-start.30) | collective-permute-done | bytes 393248 | tf_op jit(solution)/shard_map/ppermute | solution.py:233
  132.5 0.7 collective-permute-start.27
  133.2 8.9 %collective-permute-done.31 = bf16[12,128,128]{2,1,0:T(8,128)(2,1)S(1)} collective-permute-done((bf16[12,128,128]{2,1,0:T(8,128)(2,1)S(1)}, bf16[12,128,128]{2,1,0:T(8,128)(2,1)S(1)}, u32[]{:S(2)}, u32[]{:S(2)}) %collective-permute-start.31) | collective-permute-done | bytes 393248 | tf_op jit(solution)/shard_map/ppermute | solution.py:233
  142.2 0.3 fusion.5
  142.5 1.8 gather_fusion.2
  144.2 9.8 %all-to-all-start.1 = ((bf16[32,128,128]{2,1,0:T(8,128)(2,1)}), bf16[32,128,128]{2,1,0:T(8,128)(2,1)}, u32[]{:S(2)}, u32[]{:S(2)}) async-start(bf16[32,128,128]{2,1,0:T(8,128)(2,1)} %gather_fusion.2), calls=%async_computation.1 | async-start | bytes 2097152 | tf_op jit(solution)/shard_map/all_to_all | solution.py:273
  154.1 1.9 %fusion.13 = (bf16[48,4096]{1,0:T(8,128)(2,1)S(1)}, bf16[48,4096]{1,0:T(8,128)(2,1)S(1)}, bf16[48,4096]{1,0:T(8,128)(2,1)S(1)}) fusion(bf16[4,48,4096]{2,1,0:T(8,128)(2,1)} %collective-permute-done.21, bf16[4,48,4096]{2,1,0:T(8,128)(2,1)} %copy-done.5), kind=kLoop, calls=%fused_computation.32 | loop fusion | flops 2359296 | bytes 3538944 | tf_op jit(solution)/shard_map/convert_element_type | solution.py:227
  156.0 2.1 %collective-permute-start.22 = (bf16[48,4096]{1,0:T(8,128)(2,1)S(1)}, bf16[48,4096]{1,0:T(8,128)(2,1)S(1)}, u32[]{:S(2)}, u32[]{:S(2)}) collective-permute-start(bf16[48,4096]{1,0:T(8,128)(2,1)S(1)} %get-tuple-element.40), channel_id=1, source_target_pairs={{0,2},{1,3},{2,4},{3,5},{4,6},{5,7},{6,0},{7,1},{8,10},{9,11},{10,... | collective-permute-start | bytes 1179656 | tf_op jit(solution)/shard_map/ppermute | solution.py:233
  158.1 1.4 collective-permute-start.23
  159.5 1.4 collective-permute-start.24
  160.9 2.2 %fusion.8 = bf16[48,4096]{1,0:T(8,128)(2,1)} fusion(bf16[48,4096]{1,0:T(8,128)(2,1)} %collective-permute-done.28, bf16[48,4096]{1,0:T(8,128)(2,1)} %collective-permute-done.27, bf16[48,4096]{1,0:T(8,128)(2,1)S(1)} %collective-permute-done.26, bf16[4,48,4096]{2,1,0:T(8,128)(2,1)} %copy-done.14, bf16[4,48,4096]{2,1,0:T(8,128)(2,1)S(1)} %get-tuple-element.20), kind=kLoop, calls=%fused_computation.14 | loop fusion | flops 2359296 | bytes 2359296 | tf_op jit(solution)/shard_map/convert_element_type | solution.py:234
  163.1 4.6 %collective-permute-done.22 = bf16[48,4096]{1,0:T(8,128)(2,1)S(1)} collective-permute-done((bf16[48,4096]{1,0:T(8,128)(2,1)S(1)}, bf16[48,4096]{1,0:T(8,128)(2,1)S(1)}, u32[]{:S(2)}, u32[]{:S(2)}) %collective-permute-start.22) | collective-permute-done | bytes 393248 | tf_op jit(solution)/shard_map/ppermute | solution.py:233
  167.6 8.6 %collective-permute-done.23 = bf16[48,4096]{1,0:T(8,128)(2,1)S(1)} collective-permute-done((bf16[48,4096]{1,0:T(8,128)(2,1)S(1)}, bf16[48,4096]{1,0:T(8,128)(2,1)S(1)}, u32[]{:S(2)}, u32[]{:S(2)}) %collective-permute-start.23) | collective-permute-done | bytes 393248 | tf_op jit(solution)/shard_map/ppermute | solution.py:233
  176.3 2.1 %fusion.11 = bf16[48,4096]{1,0:T(8,128)(2,1)} fusion(bf16[48,4096]{1,0:T(8,128)(2,1)S(1)} %collective-permute-done.24, bf16[48,4096]{1,0:T(8,128)(2,1)S(1)} %collective-permute-done.23, bf16[48,4096]{1,0:T(8,128)(2,1)S(1)} %collective-permute-done.22, bf16[4,48,4096]{2,1,0:T(8,128)(2,1)} %collective-permute-done.21, bf16[4,48,4096]{2,1,0:T(8,128)(2,1)} %copy-done.5), kind=kLoop, calls=%fused_computation.18 | loop fusion | flops 2359296 | bytes 2359296 | tf_op jit(solution)/shard_map/convert_element_type | solution.py:234
  178.4 2.3 %all-to-all-done.1 = bf16[32,128,128]{2,1,0:T(8,128)(2,1)} async-done(((bf16[32,128,128]{2,1,0:T(8,128)(2,1)}), bf16[32,128,128]{2,1,0:T(8,128)(2,1)}, u32[]{:S(2)}, u32[]{:S(2)}) %all-to-all-start.1) | async-done | bytes 1048608 | tf_op jit(solution)/shard_map/all_to_all | solution.py:273
  180.6 1.9 %fusion = f32[4,128,128]{2,0,1:T(4,128)S(1)} fusion(s32[32]{0:T(128)S(1)} %select_reduce_fusion, pred[32]{0:T(512)(128)(4,1)S(1)} %fusion.31, bf16[4,8,128,128]{3,2,1,0:T(8,128)(2,1)} %bitcast.37), kind=kOutput, calls=%fused_computation.4 | convolution fusion | flops 4194560 | bytes 1310880 | tf_op jit(solution)/shard_map/dot_general | solution.py:279
  182.5 0.7 copy.19
  (68 shorter events, 0.4 us)
Async XLA Ops:
  0.6 1.3 copy-start
  3.6 11.9 %copy-start.6 = (bf16[48,4096]{1,0:T(8,128)(2,1)S(1)}, bf16[48,4096]{1,0:T(8,128)(2,1)}, u32[]{:S(2)}) copy-start(bf16[48,4096]{1,0:T(8,128)(2,1)} %refs_0_.1) | copy-start | bytes 1179652
  3.6 17.0 %copy-start.7 = (bf16[48,4096]{1,0:T(8,128)(2,1)S(1)}, bf16[48,4096]{1,0:T(8,128)(2,1)}, u32[]{:S(2)}) copy-start(bf16[48,4096]{1,0:T(8,128)(2,1)} %refs_8_.1) | copy-start | bytes 1179652
  3.6 35.5 %copy-start.15 = (s32[32,6,2]{0,2,1:T(2,128)S(1)}, s32[32,6,2]{0,2,1:T(2,128)}, u32[]{:S(2)}) copy-start(s32[32,6,2]{0,2,1:T(2,128)} %param.11) | copy-start | bytes 4612
  3.6 50.6 %all-to-all-start = ((bf16[32,128,128]{2,1,0:T(8,128)(2,1)}), bf16[32,128,128]{2,1,0:T(8,128)(2,1)}, u32[]{:S(2)}, u32[]{:S(2)}) async-start(bf16[32,128,128]{2,1,0:T(8,128)(2,1)} %gather_fusion), calls=%async_computation | async-start | bytes 2097152 | tf_op jit(solution)/shard_map/all_to_all | solution.py:265
  15.5 20.7 %collective-permute-start.7 = (bf16[48,4096]{1,0:T(8,128)(2,1)S(1)}, bf16[48,4096]{1,0:T(8,128)(2,1)S(1)}, u32[]{:S(2)}, u32[]{:S(2)}) collective-permute-start(bf16[48,4096]{1,0:T(8,128)(2,1)S(1)} %copy-done.6), channel_id=1, source_target_pairs={{0,2},{1,3},{2,4},{3,5},{4,6},{5,7},{6,0},{7,1},{8,10},{9,11},{10,... | collective-permute-start | bytes 1179656 | tf_op jit(solution)/shard_map/ppermute | solution.py:44
  17.1 22.0 %collective-permute-start.8 = (bf16[48,4096]{1,0:T(8,128)(2,1)S(1)}, bf16[48,4096]{1,0:T(8,128)(2,1)S(1)}, u32[]{:S(2)}, u32[]{:S(2)}) collective-permute-start(bf16[48,4096]{1,0:T(8,128)(2,1)S(1)} %copy-done.6), channel_id=1, source_target_pairs={{0,6},{1,7},{2,0},{3,1},{4,2},{5,3},{6,4},{7,5},{8,14},{9,15},{10,... | collective-permute-start | bytes 1179656 | tf_op jit(solution)/shard_map/ppermute | solution.py:44
  18.8 20.3 %collective-permute-start.9 = (bf16[48,4096]{1,0:T(8,128)(2,1)S(1)}, bf16[48,4096]{1,0:T(8,128)(2,1)S(1)}, u32[]{:S(2)}, u32[]{:S(2)}) collective-permute-start(bf16[48,4096]{1,0:T(8,128)(2,1)S(1)} %copy-done.6), channel_id=1, source_target_pairs={{0,4},{1,5},{2,6},{3,7},{4,0},{5,1},{6,2},{7,3},{8,12},{9,13},{10,... | collective-permute-start | bytes 1179656 | tf_op jit(solution)/shard_map/ppermute | solution.py:44
  20.6 24.1 %collective-permute-start.14 = (bf16[48,4096]{1,0:T(8,128)(2,1)S(1)}, bf16[48,4096]{1,0:T(8,128)(2,1)}, u32[]{:S(2)}, u32[]{:S(2)}) collective-permute-start(bf16[48,4096]{1,0:T(8,128)(2,1)S(1)} %copy-done.7), channel_id=1, source_target_pairs={{0,2},{1,3},{2,4},{3,5},{4,6},{5,7},{6,0},{7,1},{8,10},{9,11},{10,... | collective-permute-start | bytes 1179656 | tf_op jit(solution)/shard_map/ppermute | solution.py:44
  21.2 24.8 %collective-permute-start.15 = (bf16[48,4096]{1,0:T(8,128)(2,1)S(1)}, bf16[48,4096]{1,0:T(8,128)(2,1)S(1)}, u32[]{:S(2)}, u32[]{:S(2)}) collective-permute-start(bf16[48,4096]{1,0:T(8,128)(2,1)S(1)} %copy-done.7), channel_id=1, source_target_pairs={{0,6},{1,7},{2,0},{3,1},{4,2},{5,3},{6,4},{7,5},{8,14},{9,15},{10,... | collective-permute-start | bytes 1179656 | tf_op jit(solution)/shard_map/ppermute | solution.py:44
  36.2 17.3 %collective-permute-start.16 = (bf16[48,4096]{1,0:T(8,128)(2,1)S(1)}, bf16[48,4096]{1,0:T(8,128)(2,1)}, u32[]{:S(2)}, u32[]{:S(2)}) collective-permute-start(bf16[48,4096]{1,0:T(8,128)(2,1)S(1)} %copy-done.7), channel_id=1, source_target_pairs={{0,4},{1,5},{2,6},{3,7},{4,0},{5,1},{6,2},{7,3},{8,12},{9,13},{10,... | collective-permute-start | bytes 1179656 | tf_op jit(solution)/shard_map/ppermute | solution.py:44
  39.1 14.6 %collective-permute-start.10 = (bf16[48,4096]{1,0:T(8,128)(2,1)S(1)}, bf16[48,4096]{1,0:T(8,128)(2,1)}, u32[]{:S(2)}, u32[]{:S(2)}) collective-permute-start(bf16[48,4096]{1,0:T(8,128)(2,1)S(1)} %copy-done.6), channel_id=1, source_target_pairs={{0,1},{1,0},{2,3},{3,2},{4,5},{5,4},{6,7},{7,6},{8,9},{9,8},{10,11... | collective-permute-start | bytes 1179656 | tf_op jit(solution)/shard_map/ppermute | solution.py:45
  39.1 17.0 %collective-permute-start.17 = (bf16[48,4096]{1,0:T(8,128)(2,1)S(1)}, bf16[48,4096]{1,0:T(8,128)(2,1)}, u32[]{:S(2)}, u32[]{:S(2)}) collective-permute-start(bf16[48,4096]{1,0:T(8,128)(2,1)S(1)} %copy-done.7), channel_id=1, source_target_pairs={{0,1},{1,0},{2,3},{3,2},{4,5},{5,4},{6,7},{7,6},{8,9},{9,8},{10,11... | collective-permute-start | bytes 1179656 | tf_op jit(solution)/shard_map/ppermute | solution.py:45
  44.8 11.4 %collective-permute-start.11 = (bf16[48,4096]{1,0:T(8,128)(2,1)S(1)}, bf16[48,4096]{1,0:T(8,128)(2,1)}, u32[]{:S(2)}, u32[]{:S(2)}) collective-permute-start(bf16[48,4096]{1,0:T(8,128)(2,1)S(1)} %collective-permute-done.7.refs_1_), channel_id=1, source_target_pairs={{0,1},{1,0},{2,3},{3,2},{4,5},{5,4},{6,7},{7,6},{8,9},{9,8},{10,11... | collective-permute-start | bytes 1179656 | tf_op jit(solution)/shard_map/ppermute | solution.py:45
  46.0 8.2 %copy-start.8 = (bf16[48,4096]{1,0:T(8,128)(2,1)}, bf16[48,4096]{1,0:T(8,128)(2,1)S(1)}, u32[]{:S(2)}) copy-start(bf16[48,4096]{1,0:T(8,128)(2,1)S(1)} %collective-permute-done.15.refs_10_) | copy-start | bytes 1179652
  46.0 11.4 %collective-permute-start.12 = (bf16[48,4096]{1,0:T(8,128)(2,1)S(1)}, bf16[48,4096]{1,0:T(8,128)(2,1)}, u32[]{:S(2)}, u32[]{:S(2)}) collective-permute-start(bf16[48,4096]{1,0:T(8,128)(2,1)S(1)} %collective-permute-done.8.refs_2_), channel_id=1, source_target_pairs={{0,1},{1,0},{2,3},{3,2},{4,5},{5,4},{6,7},{7,6},{8,9},{9,8},{10,11... | collective-permute-start | bytes 1179656 | tf_op jit(solution)/shard_map/ppermute | solution.py:45
  53.5 6.0 %collective-permute-start.13 = (bf16[48,4096]{1,0:T(8,128)(2,1)S(1)}, bf16[48,4096]{1,0:T(8,128)(2,1)}, u32[]{:S(2)}, u32[]{:S(2)}) collective-permute-start(bf16[48,4096]{1,0:T(8,128)(2,1)S(1)} %collective-permute-done.9.refs_3_), channel_id=1, source_target_pairs={{0,1},{1,0},{2,3},{3,2},{4,5},{5,4},{6,7},{7,6},{8,9},{9,8},{10,11... | collective-permute-start | bytes 1179656 | tf_op jit(solution)/shard_map/ppermute | solution.py:45
  53.7 6.4 %collective-permute-start.18 = (bf16[48,4096]{1,0:T(8,128)(2,1)}, bf16[48,4096]{1,0:T(8,128)(2,1)}, u32[]{:S(2)}, u32[]{:S(2)}) collective-permute-start(bf16[48,4096]{1,0:T(8,128)(2,1)} %collective-permute-done.14.refs_9_), channel_id=1, source_target_pairs={{0,1},{1,0},{2,3},{3,2},{4,5},{5,4},{6,7},{7,6},{8,9},{9,8},{10,11... | collective-permute-start | bytes 1179656 | tf_op jit(solution)/shard_map/ppermute | solution.py:45
  56.1 4.0 %collective-permute-start.19 = (bf16[48,4096]{1,0:T(8,128)(2,1)}, bf16[48,4096]{1,0:T(8,128)(2,1)S(1)}, u32[]{:S(2)}, u32[]{:S(2)}) collective-permute-start(bf16[48,4096]{1,0:T(8,128)(2,1)} %copy-done.8), channel_id=1, source_target_pairs={{0,1},{1,0},{2,3},{3,2},{4,5},{5,4},{6,7},{7,6},{8,9},{9,8},{10,11... | collective-permute-start | bytes 1179656 | tf_op jit(solution)/shard_map/ppermute | solution.py:45
  56.2 13.5 %collective-permute-start = (bf16[12,128,128]{2,1,0:T(8,128)(2,1)S(1)}, bf16[12,128,128]{2,1,0:T(8,128)(2,1)}, u32[]{:S(2)}, u32[]{:S(2)}) collective-permute-start(bf16[12,128,128]{2,1,0:T(8,128)(2,1)S(1)} %gather_fusion.1), channel_id=1, source_target_pairs={{0,2},{1,3},{2,4},{3,5},{4,6},{5,7},{6,0},{7,1},{8,10},{9,11},{10,... | collective-permute-start | bytes 1179656 | tf_op jit(solution)/shard_map/ppermute | solution.py:44
  57.4 19.2 %collective-permute-start.1 = (bf16[12,128,128]{2,1,0:T(8,128)(2,1)S(1)}, bf16[12,128,128]{2,1,0:T(8,128)(2,1)}, u32[]{:S(2)}, u32[]{:S(2)}) collective-permute-start(bf16[12,128,128]{2,1,0:T(8,128)(2,1)S(1)} %gather_fusion.1), channel_id=1, source_target_pairs={{0,6},{1,7},{2,0},{3,1},{4,2},{5,3},{6,4},{7,5},{8,14},{9,15},{10,... | collective-permute-start | bytes 1179656 | tf_op jit(solution)/shard_map/ppermute | solution.py:44
  59.5 18.1 %collective-permute-start.2 = (bf16[12,128,128]{2,1,0:T(8,128)(2,1)S(1)}, bf16[12,128,128]{2,1,0:T(8,128)(2,1)}, u32[]{:S(2)}, u32[]{:S(2)}) collective-permute-start(bf16[12,128,128]{2,1,0:T(8,128)(2,1)S(1)} %gather_fusion.1), channel_id=1, source_target_pairs={{0,4},{1,5},{2,6},{3,7},{4,0},{5,1},{6,2},{7,3},{8,12},{9,13},{10,... | collective-permute-start | bytes 1179656 | tf_op jit(solution)/shard_map/ppermute | solution.py:44
  60.1 17.7 %collective-permute-start.20 = (bf16[48,4096]{1,0:T(8,128)(2,1)}, bf16[48,4096]{1,0:T(8,128)(2,1)}, u32[]{:S(2)}, u32[]{:S(2)}) collective-permute-start(bf16[48,4096]{1,0:T(8,128)(2,1)} %collective-permute-done.16.refs_11_), channel_id=1, source_target_pairs={{0,1},{1,0},{2,3},{3,2},{4,5},{5,4},{6,7},{7,6},{8,9},{9,8},{10,11... | collective-permute-start | bytes 1179656 | tf_op jit(solution)/shard_map/ppermute | solution.py:45
  60.1 0.7 copy-start.10
  60.8 31.9 %collective-permute-start.3 = (bf16[12,128,128]{2,1,0:T(8,128)(2,1)S(1)}, bf16[12,128,128]{2,1,0:T(8,128)(2,1)}, u32[]{:S(2)}, u32[]{:S(2)}) collective-permute-start(bf16[12,128,128]{2,1,0:T(8,128)(2,1)S(1)} %gather_fusion.1), channel_id=1, source_target_pairs={{0,1},{1,0},{2,3},{3,2},{4,5},{5,4},{6,7},{7,6},{8,9},{9,8},{10,11... | collective-permute-start | bytes 1179656 | tf_op jit(solution)/shard_map/ppermute | solution.py:45
  69.7 23.0 %collective-permute-start.4 = (bf16[12,128,128]{2,1,0:T(8,128)(2,1)}, bf16[12,128,128]{2,1,0:T(8,128)(2,1)}, u32[]{:S(2)}, u32[]{:S(2)}) collective-permute-start(bf16[12,128,128]{2,1,0:T(8,128)(2,1)} %collective-permute-done.refs_1_), channel_id=1, source_target_pairs={{0,1},{1,0},{2,3},{3,2},{4,5},{5,4},{6,7},{7,6},{8,9},{9,8},{10,11... | collective-permute-start | bytes 1179656 | tf_op jit(solution)/shard_map/ppermute | solution.py:45
  76.7 16.1 %collective-permute-start.5 = (bf16[12,128,128]{2,1,0:T(8,128)(2,1)}, bf16[12,128,128]{2,1,0:T(8,128)(2,1)}, u32[]{:S(2)}, u32[]{:S(2)}) collective-permute-start(bf16[12,128,128]{2,1,0:T(8,128)(2,1)} %collective-permute-done.1.refs_2_), channel_id=1, source_target_pairs={{0,1},{1,0},{2,3},{3,2},{4,5},{5,4},{6,7},{7,6},{8,9},{9,8},{10,11... | collective-permute-start | bytes 1179656 | tf_op jit(solution)/shard_map/ppermute | solution.py:45
  77.6 15.2 %collective-permute-start.6 = (bf16[12,128,128]{2,1,0:T(8,128)(2,1)}, bf16[12,128,128]{2,1,0:T(8,128)(2,1)}, u32[]{:S(2)}, u32[]{:S(2)}) collective-permute-start(bf16[12,128,128]{2,1,0:T(8,128)(2,1)} %collective-permute-done.2.refs_3_), channel_id=1, source_target_pairs={{0,1},{1,0},{2,3},{3,2},{4,5},{5,4},{6,7},{7,6},{8,9},{9,8},{10,11... | collective-permute-start | bytes 1179656 | tf_op jit(solution)/shard_map/ppermute | solution.py:45
  77.8 2.2 %copy-start.1 = (bf16[4096,512]{1,0:T(8,128)(2,1)S(1)}, bf16[4096,512]{1,0:T(8,128)(2,1)}, u32[]{:S(2)}) copy-start(bf16[4096,512]{1,0:T(8,128)(2,1)} %w_ref.3) | copy-start | bytes 12582916
  80.0 2.2 %copy-start.3 = (bf16[512,4096]{1,0:T(8,128)(2,1)S(1)}, bf16[512,4096]{1,0:T(8,128)(2,1)}, u32[]{:S(2)}) copy-start(bf16[512,4096]{1,0:T(8,128)(2,1)} %w_ref.2) | copy-start | bytes 12582916
  82.2 1.0 copy-start.9
  83.2 1.0 copy-start.11
  84.2 8.6 %copy-start.12 = (bf16[1024,512]{1,0:T(8,128)(2,1)S(1)}, bf16[1024,512]{1,0:T(8,128)(2,1)}, u32[]{:S(2)}) copy-start(bf16[1024,512]{1,0:T(8,128)(2,1)} %refs_10_.1) | copy-start | bytes 3145732
  84.2 8.6 %copy-start.13 = (bf16[1024,512]{1,0:T(8,128)(2,1)S(1)}, bf16[1024,512]{1,0:T(8,128)(2,1)}, u32[]{:S(2)}) copy-start(bf16[1024,512]{1,0:T(8,128)(2,1)} %refs_11_.1) | copy-start | bytes 3145732
  92.8 17.0 %copy-start.2 = (bf16[4096,512]{1,0:T(8,128)(2,1)S(1)}, bf16[4096,512]{1,0:T(8,128)(2,1)}, u32[]{:S(2)}) copy-start(bf16[4096,512]{1,0:T(8,128)(2,1)} %w_ref.3) | copy-start | bytes 12582916
  109.2 9.1 %collective-permute-start.29 = (bf16[4,12,128,128]{3,2,1,0:T(8,128)(2,1)S(1)}, bf16[4,12,128,128]{3,2,1,0:T(8,128)(2,1)S(1)}, u32[]{:S(2)}, u32[]{:S(2)}) collective-permute-start(bf16[4,12,128,128]{3,2,1,0:T(8,128)(2,1)S(1)} %get-tuple-element.23), channel_id=1, source_target_pairs={{0,1},{1,0},{2,3},{3,2},{4,5},{5,4},{6,7},{7,6},{8,9},{9,8},{10,11... | collective-permute-start | bytes 4718600 | tf_op jit(solution)/shard_map/ppermute | solution.py:226
  109.8 3.9 %copy-start.4 = (bf16[512,4096]{1,0:T(8,128)(2,1)S(1)}, bf16[512,4096]{1,0:T(8,128)(2,1)}, u32[]{:S(2)}) copy-start(bf16[512,4096]{1,0:T(8,128)(2,1)} %w_ref.2) | copy-start | bytes 12582916
  113.0 10.8 %collective-permute-start.25 = (bf16[4,48,4096]{2,1,0:T(8,128)(2,1)S(1)}, bf16[4,48,4096]{2,1,0:T(8,128)(2,1)S(1)}, u32[]{:S(2)}, u32[]{:S(2)}) collective-permute-start(bf16[4,48,4096]{2,1,0:T(8,128)(2,1)S(1)} %get-tuple-element.21), channel_id=1, source_target_pairs={{0,1},{1,0},{2,3},{3,2},{4,5},{5,4},{6,7},{7,6},{8,9},{9,8},{10,11... | collective-permute-start | bytes 4718600 | tf_op jit(solution)/shard_map/ppermute | solution.py:226
  117.8 1.2 copy-start.5
  117.8 36.3 %collective-permute-start.21 = (bf16[4,48,4096]{2,1,0:T(8,128)(2,1)}, bf16[4,48,4096]{2,1,0:T(8,128)(2,1)}, u32[]{:S(2)}, u32[]{:S(2)}) collective-permute-start(bf16[4,48,4096]{2,1,0:T(8,128)(2,1)} %get-tuple-element.18), channel_id=1, source_target_pairs={{0,1},{1,0},{2,3},{3,2},{4,5},{5,4},{6,7},{7,6},{8,9},{9,8},{10,11... | collective-permute-start | bytes 4718600 | tf_op jit(solution)/shard_map/ppermute | solution.py:226
  119.0 13.5 %collective-permute-start.30 = (bf16[12,128,128]{2,1,0:T(8,128)(2,1)S(1)}, bf16[12,128,128]{2,1,0:T(8,128)(2,1)S(1)}, u32[]{:S(2)}, u32[]{:S(2)}) collective-permute-start(bf16[12,128,128]{2,1,0:T(8,128)(2,1)S(1)} %get-tuple-element.34), channel_id=1, source_target_pairs={{0,2},{1,3},{2,4},{3,5},{4,6},{5,7},{6,0},{7,1},{8,10},{9,11},{10,... | collective-permute-start | bytes 1179656 | tf_op jit(solution)/shard_map/ppermute | solution.py:233
  120.1 22.1 %collective-permute-start.31 = (bf16[12,128,128]{2,1,0:T(8,128)(2,1)S(1)}, bf16[12,128,128]{2,1,0:T(8,128)(2,1)S(1)}, u32[]{:S(2)}, u32[]{:S(2)}) collective-permute-start(bf16[12,128,128]{2,1,0:T(8,128)(2,1)S(1)} %get-tuple-element.36), channel_id=1, source_target_pairs={{0,4},{1,5},{2,6},{3,7},{4,0},{5,1},{6,2},{7,3},{8,12},{9,13},{10,... | collective-permute-start | bytes 1179656 | tf_op jit(solution)/shard_map/ppermute | solution.py:233
  123.8 18.4 %collective-permute-start.32 = (bf16[12,128,128]{2,1,0:T(8,128)(2,1)S(1)}, bf16[12,128,128]{2,1,0:T(8,128)(2,1)S(1)}, u32[]{:S(2)}, u32[]{:S(2)}) collective-permute-start(bf16[12,128,128]{2,1,0:T(8,128)(2,1)S(1)} %get-tuple-element.35), channel_id=1, source_target_pairs={{0,6},{1,7},{2,0},{3,1},{4,2},{5,3},{6,4},{7,5},{8,14},{9,15},{10,... | collective-permute-start | bytes 1179656 | tf_op jit(solution)/shard_map/ppermute | solution.py:233
  123.8 1.6 copy-start.14
  125.4 34.1 %collective-permute-start.26 = (bf16[48,4096]{1,0:T(8,128)(2,1)}, bf16[48,4096]{1,0:T(8,128)(2,1)S(1)}, u32[]{:S(2)}, u32[]{:S(2)}) collective-permute-start(bf16[48,4096]{1,0:T(8,128)(2,1)} %get-tuple-element.37), channel_id=1, source_target_pairs={{0,2},{1,3},{2,4},{3,5},{4,6},{5,7},{6,0},{7,1},{8,10},{9,11},{10,... | collective-permute-start | bytes 1179656 | tf_op jit(solution)/shard_map/ppermute | solution.py:233
  132.5 28.3 %collective-permute-start.27 = (bf16[48,4096]{1,0:T(8,128)(2,1)}, bf16[48,4096]{1,0:T(8,128)(2,1)}, u32[]{:S(2)}, u32[]{:S(2)}) collective-permute-start(bf16[48,4096]{1,0:T(8,128)(2,1)} %get-tuple-element.39), channel_id=1, source_target_pairs={{0,4},{1,5},{2,6},{3,7},{4,0},{5,1},{6,2},{7,3},{8,12},{9,13},{10,... | collective-permute-start | bytes 1179656 | tf_op jit(solution)/shard_map/ppermute | solution.py:233
  142.2 18.7 %collective-permute-start.28 = (bf16[48,4096]{1,0:T(8,128)(2,1)}, bf16[48,4096]{1,0:T(8,128)(2,1)}, u32[]{:S(2)}, u32[]{:S(2)}) collective-permute-start(bf16[48,4096]{1,0:T(8,128)(2,1)} %get-tuple-element.38), channel_id=1, source_target_pairs={{0,6},{1,7},{2,0},{3,1},{4,2},{5,3},{6,4},{7,5},{8,14},{9,15},{10,... | collective-permute-start | bytes 1179656 | tf_op jit(solution)/shard_map/ppermute | solution.py:233
  144.2 36.4 %all-to-all-start.1 = ((bf16[32,128,128]{2,1,0:T(8,128)(2,1)}), bf16[32,128,128]{2,1,0:T(8,128)(2,1)}, u32[]{:S(2)}, u32[]{:S(2)}) async-start(bf16[32,128,128]{2,1,0:T(8,128)(2,1)} %gather_fusion.2), calls=%async_computation.1 | async-start | bytes 2097152 | tf_op jit(solution)/shard_map/all_to_all | solution.py:273
  156.0 11.7 %collective-permute-start.22 = (bf16[48,4096]{1,0:T(8,128)(2,1)S(1)}, bf16[48,4096]{1,0:T(8,128)(2,1)S(1)}, u32[]{:S(2)}, u32[]{:S(2)}) collective-permute-start(bf16[48,4096]{1,0:T(8,128)(2,1)S(1)} %get-tuple-element.40), channel_id=1, source_target_pairs={{0,2},{1,3},{2,4},{3,5},{4,6},{5,7},{6,0},{7,1},{8,10},{9,11},{10,... | collective-permute-start | bytes 1179656 | tf_op jit(solution)/shard_map/ppermute | solution.py:233
  158.1 18.2 %collective-permute-start.23 = (bf16[48,4096]{1,0:T(8,128)(2,1)S(1)}, bf16[48,4096]{1,0:T(8,128)(2,1)S(1)}, u32[]{:S(2)}, u32[]{:S(2)}) collective-permute-start(bf16[48,4096]{1,0:T(8,128)(2,1)S(1)} %get-tuple-element.42), channel_id=1, source_target_pairs={{0,4},{1,5},{2,6},{3,7},{4,0},{5,1},{6,2},{7,3},{8,12},{9,13},{10,... | collective-permute-start | bytes 1179656 | tf_op jit(solution)/shard_map/ppermute | solution.py:233
  159.5 16.8 %collective-permute-start.24 = (bf16[48,4096]{1,0:T(8,128)(2,1)S(1)}, bf16[48,4096]{1,0:T(8,128)(2,1)S(1)}, u32[]{:S(2)}, u32[]{:S(2)}) collective-permute-start(bf16[48,4096]{1,0:T(8,128)(2,1)S(1)} %get-tuple-element.41), channel_id=1, source_target_pairs={{0,6},{1,7},{2,0},{3,1},{4,2},{5,3},{6,4},{7,5},{8,14},{9,15},{10,... | collective-permute-start | bytes 1179656 | tf_op jit(solution)/shard_map/ppermute | solution.py:233
